TPU v7x, 512 devices: a whole 4x8x8 slice. The times are simulated.
512 devices in a mesh: dp: 16 (over z, core), ctx: 32 (over y, x).
Axes of the slice: x: 4, y: 8, z: 8, core: 2. Of those that a mesh axis runs over, the one named last changes fastest.
Arguments:
- queries: bfloat16 [16, 4096, 2560], P('dp', 'ctx'), may hold values from -6 to 6
- keys: bfloat16 [16, 4096, 512], P('dp', 'ctx'), may hold values from -6 to 6
- values: bfloat16 [16, 4096, 512], P('dp', 'ctx'), may hold values from -6 to 6
- outputs: bfloat16 [16, 4096, 2560], P('dp', 'ctx'), may hold values from -6 to 6
- d_out: bfloat16 [16, 4096, 2560], P('dp', 'ctx'), may hold values from -6 to 6
- log_sums: float32 [16, 20, 4096], P('dp', None, 'ctx'), may hold values from 2 to 6
- block_path: int32 [16, 32], P('dp'), may hold values from 0 to 16, as said below
- live_len: int32 [16, 32], P('dp'), may hold values from 1 to 128, as said below
Outputs:
- grad_query: bfloat16 [16, 4096, 2560], P('dp', 'ctx')
- grad_key: bfloat16 [16, 4096, 512], P('dp', 'ctx')
- grad_value: bfloat16 [16, 4096, 512], P('dp', 'ctx')
- bias_grad: float32 [1024], P('dp')
Inputs may be any that keep to these rules, and one draw needn't show every extreme that they name: `block_path`: for each sequence: one or two shared opening blocks and one or two shared closing blocks; the blocks between form 8 to 16 consecutive runs numbered 1, 2, ... in order, one run a path; some sequence has 16 paths. `live_len`: only the last block of a path may be partly live; every other block is full.
All inputs are finite; a program needn't handle non-finite values.
Results may differ from a plain program's by a relative error of at most 0.015.
Values may be sent and summed in bfloat16 or wider, within the bound.
A program may use at most 128 MiB of HBM per device.

v0:
```python
import functools

import jax
import jax.numpy as jnp
from jax import lax
from jax.sharding import PartitionSpec as P

QUERY_HEAD_COUNT = 20
KEY_VALUE_HEADS = 4
HEAD_WIDTH = 128
BLK = 128


def visible(query_pos, key_pos, block_paths, live_counts, block_size):
    slots = jnp.arange(block_paths.shape[0], dtype=jnp.int32)
    shared = lax.cummax(jnp.where(block_paths == 0, slots, -1), axis=0)
    query_block = query_pos // block_size
    key_block = key_pos // block_size
    query_hot = (query_block[:, None] == slots[None, :]).astype(jnp.int32)
    key_hot = (key_block[:, None] == slots[None, :]).astype(jnp.int32)
    query_path = jnp.sum(query_hot * block_paths[None, :], axis=1)
    query_last = jnp.sum(query_hot * shared[None, :], axis=1)
    key_path = jnp.sum(key_hot * block_paths[None, :], axis=1)
    key_live = jnp.sum(key_hot * live_counts[None, :], axis=1)
    causal = key_pos[None, :] <= query_pos[:, None]
    filled = key_pos % block_size < key_live
    joined = (
        (key_path == 0)[None, :]
        | (key_path[None, :] == query_path[:, None])
        | (query_last[:, None] > key_block[None, :])
    )
    return causal & filled[None, :] & joined


def key_terms(
    query_tile,
    grad_tile,
    log_tile,
    delta_tile,
    work_pos,
    block_paths,
    live_counts,
    score_scale,
    carry,
    pieces,
    start,
):
    key_piece, value_piece = pieces
    piece_rows = key_piece.shape[0]
    heads_each_pass = query_tile.shape[1]
    tile_rows = 512

    def one_tile(tile_turn, state):
        offset = tile_turn * tile_rows
        key_tile = lax.dynamic_slice_in_dim(key_piece, offset, tile_rows, 0).reshape(
            tile_rows, heads_each_pass, HEAD_WIDTH
        )
        value_tile = lax.dynamic_slice_in_dim(value_piece, offset, tile_rows, 0).reshape(
            tile_rows, heads_each_pass, HEAD_WIDTH
        )
        key_pos = offset + jnp.arange(tile_rows, dtype=jnp.int32)
        allowed = visible(work_pos, key_pos, block_paths, live_counts, BLK)

        def compute(inner):
            grad_query, key_value = inner
            scores = (
                jnp.einsum(
                    "qcgd,kcd->qcgk", query_tile, key_tile, preferred_element_type=jnp.float32
                )
                * score_scale
            )
            weights_full = jnp.where(
                allowed[:, None, None, :], jnp.exp(scores - log_tile[..., None]), 0.0
            )
            weights_low = weights_full.astype(jnp.bfloat16)
            value_part = jnp.einsum(
                "qcgk,qcgd->kcd", weights_low, grad_tile, preferred_element_type=jnp.float32
            )
            grad_weights = jnp.einsum(
                "qcgd,kcd->qcgk", grad_tile, value_tile, preferred_element_type=jnp.float32
            )
            grad_scores = (
                weights_full * (grad_weights - delta_tile[..., None]) * score_scale
            ).astype(jnp.bfloat16)
            grad_query = grad_query + jnp.einsum(
                "qcgk,kcd->qcgd", grad_scores, key_tile, preferred_element_type=jnp.float32
            )
            key_part = jnp.einsum(
                "qcgk,qcgd->kcd", grad_scores, query_tile, preferred_element_type=jnp.float32
            )
            update = jnp.stack(
                [key_part.reshape(tile_rows, -1), value_part.reshape(tile_rows, -1)], axis=1
            )
            current = lax.dynamic_slice_in_dim(key_value, offset, tile_rows, 0)
            key_value = lax.dynamic_update_slice_in_dim(key_value, current + update, offset, 0)
            return (grad_query, key_value)

        def unchanged(inner):
            return inner

        return lax.cond(jnp.any(allowed), compute, unchanged, state)

    return lax.fori_loop(0, piece_rows // tile_rows, one_tile, carry)


def on_device(queries, keys, values, outputs, d_out, log_sums, block_path, live_len):
    devices = lax.axis_size("ctx")
    position = lax.axis_index("ctx")
    local_rows = queries.shape[1]
    sequence_length = local_rows * devices
    group_width = QUERY_HEAD_COUNT // KEY_VALUE_HEADS
    score_scale = HEAD_WIDTH ** (-0.5)
    block_paths = block_path[0]
    live_counts = live_len[0]
    query_heads = queries[0].reshape(local_rows, QUERY_HEAD_COUNT, HEAD_WIDTH)
    grad_heads = d_out[0].reshape(local_rows, QUERY_HEAD_COUNT, HEAD_WIDTH)
    deltas = jnp.sum(
        grad_heads.astype(jnp.float32)
        * outputs[0].reshape(local_rows, QUERY_HEAD_COUNT, HEAD_WIDTH).astype(jnp.float32),
        axis=2,
    )
    log_sum = jnp.transpose(log_sums[0])
    own_pos = position * local_rows + jnp.arange(local_rows, dtype=jnp.int32)
    total_rows = query_heads.shape[0]
    heads_each_pass = 1
    width = heads_each_pass * HEAD_WIDTH
    query_grads = []
    key_grads = []
    value_grads = []
    for leading_head in range(0, KEY_VALUE_HEADS, heads_each_pass):
        head_lower = leading_head * group_width
        head_upper = head_lower + heads_each_pass * group_width
        query_tile = query_heads[:, head_lower:head_upper].reshape(
            total_rows, heads_each_pass, group_width, HEAD_WIDTH
        )
        grad_tile = grad_heads[:, head_lower:head_upper].reshape(
            total_rows, heads_each_pass, group_width, HEAD_WIDTH
        )
        log_tile = log_sum[:, head_lower:head_upper].reshape(
            total_rows, heads_each_pass, group_width
        )
        delta_tile = deltas[:, head_lower:head_upper].reshape(
            total_rows, heads_each_pass, group_width
        )
        fold_keys = functools.partial(
            key_terms,
            query_tile,
            grad_tile,
            log_tile,
            delta_tile,
            own_pos,
            block_paths,
            live_counts,
            score_scale,
        )
        start_state = (
            jnp.zeros((total_rows, heads_each_pass, group_width, HEAD_WIDTH), jnp.float32),
            jnp.zeros((sequence_length, 2, width), jnp.float32),
        )
        key_slice = keys[0][:, leading_head * HEAD_WIDTH : leading_head * HEAD_WIDTH + width]
        value_slice = values[0][:, leading_head * HEAD_WIDTH : leading_head * HEAD_WIDTH + width]
        query_part, partial_value = fold_keys(
            start_state,
            (
                lax.all_gather(key_slice, "ctx", axis=0, tiled=True),
                lax.all_gather(value_slice, "ctx", axis=0, tiled=True),
            ),
            jnp.int32(0),
        )
        shares = partial_value.astype(jnp.bfloat16).reshape(devices, local_rows, 2, width)
        arrived = lax.all_to_all(shares, "ctx", split_axis=0, concat_axis=0, tiled=True)
        summed = jnp.sum(arrived.astype(jnp.float32), axis=0)
        query_grads.append(
            query_part.reshape(total_rows, heads_each_pass * group_width * HEAD_WIDTH)
        )
        key_grads.append(summed[:, 0])
        value_grads.append(summed[:, 1])
    query_full = jnp.concatenate(query_grads, axis=1)
    grad_query = query_full.astype(jnp.bfloat16)
    key_full = jnp.concatenate(key_grads, axis=1)
    value_full = jnp.concatenate(value_grads, axis=1)
    column_sums = jnp.concatenate([jnp.sum(key_full, axis=0), jnp.sum(value_full, axis=0)])
    across = lax.psum(column_sums, "ctx")
    bias_share = lax.psum_scatter(across, "dp", scatter_dimension=0, tiled=True)
    return (
        grad_query[None],
        key_full.astype(jnp.bfloat16)[None],
        value_full.astype(jnp.bfloat16)[None],
        bias_share,
    )


def solution(mesh):
    return jax.shard_map(
        on_device,
        mesh=mesh,
        in_specs=(
            P("dp", "ctx", None),
            P("dp", "ctx", None),
            P("dp", "ctx", None),
            P("dp", "ctx", None),
            P("dp", "ctx", None),
            P("dp", None, "ctx"),
            P("dp", None),
            P("dp", None),
        ),
        out_specs=(P("dp", "ctx", None), P("dp", "ctx", None), P("dp", "ctx", None), P("dp")),
        check_vma=False,
    )
```

profile of v0, /device:TPU:32, one launch (start us, length us, event | category | flops | bytes accessed | tf_op | source)
XLA Modules:
  0.0 926.7 jit_solution(2220076931224658794)
XLA Ops:
  21.0 73.9 %all-gather.11.cloned.1.call-done = bf16[4096,128]{1,0:T(8,128)(2,1)} async-done(((bf16[128,128]{1,0:T(8,128)(2,1)}), bf16[4096,128]{1,0:T(8,128)(2,1)}) %all-gather.11.cloned.1.call-update) | async-done | bytes 1048592 | tf_op jit(solution)/shard_map/all_gather | solution.py:166
  94.9 83.2 %all-gather.9.cloned.1.call-done = bf16[4096,128]{1,0:T(8,128)(2,1)} async-done(((bf16[128,128]{1,0:T(8,128)(2,1)}), bf16[4096,128]{1,0:T(8,128)(2,1)}) %all-gather.9.cloned.1.call-update) | async-done | bytes 1048592 | tf_op jit(solution)/shard_map/all_gather | solution.py:165
  180.4 36.6 %while.84 = (s32[]{:T(128)}, f32[128,1,5,128]{0,3,2,1:T(8,128)S(1)}, f32[4096,2,128]{2,0,1:T(8,128)}, s32[1,32]{1,0:T(1,128)S(1)}, s32[1,32]{1,0:T(1,128)S(1)}, ...) while((s32[]{:T(128)}, ...), condition=%wide.region_10.11_spmd.clone.clone, body=%wide.region_2.10_spmd.clone.clone.sunk | while | flops 423038848 | bytes 9862997 | solution.py:103
  182.5 6.5 conditional.16
  195.4 6.5 conditional.16
  220.9 38.9 %all-to-all-start = ((bf16[32,128,2,128]{3,1,2,0:T(8,128)(2,1)}), bf16[32,128,2,128]{3,1,2,0:T(8,128)(2,1)S(1)}, u32[]{:S(2)}, u32[]{:S(2)}) async-start(bf16[32,128,2,128]{3,1,2,0:T(8,128)(2,1)} %copy.107), calls=%async_computation | async-start | bytes 4194304 | tf_op jit(solution)/shard_map/all_to_all | solution.py:171
  264.4 85.4 %all-gather.15.cloned.1.call-done = bf16[4096,128]{1,0:T(8,128)(2,1)} async-done(((bf16[128,128]{1,0:T(8,128)(2,1)}), bf16[4096,128]{1,0:T(8,128)(2,1)}) %all-gather.15.cloned.1.call-update) | async-done | bytes 1048592 | tf_op jit(solution)/shard_map/all_gather | solution.py:166
  352.0 36.5 %while.85 = (s32[]{:T(128)}, f32[128,1,5,128]{0,3,2,1:T(8,128)S(1)}, f32[4096,2,128]{2,0,1:T(8,128)}, s32[1,32]{1,0:T(1,128)S(1)}, s32[1,32]{1,0:T(1,128)S(1)}, ...) while((s32[]{:T(128)}, ...), condition=%wide.region_19.20_spmd.clone.clone, body=%wide.region_11.19_spmd.clone.clone.sunk | while | flops 423038848 | bytes 9862997 | solution.py:103
  354.1 6.5 conditional.17
  367.0 6.5 conditional.17
  393.8 38.9 %all-to-all-start.1 = ((bf16[32,128,2,128]{3,1,2,0:T(8,128)(2,1)}), bf16[32,128,2,128]{3,1,2,0:T(8,128)(2,1)}, u32[]{:S(2)}, u32[]{:S(2)}) async-start(bf16[32,128,2,128]{3,1,2,0:T(8,128)(2,1)} %copy.108), calls=%async_computation.1 | async-start | bytes 4194304 | tf_op jit(solution)/shard_map/all_to_all | solution.py:171
  432.8 89.7 %all-gather.19.cloned.1.call-done = bf16[4096,128]{1,0:T(8,128)(2,1)} async-done(((bf16[128,128]{1,0:T(8,128)(2,1)}), bf16[4096,128]{1,0:T(8,128)(2,1)}) %all-gather.19.cloned.1.call-update) | async-done | bytes 1048592 | tf_op jit(solution)/shard_map/all_gather | solution.py:166
  524.7 36.5 %while.86 = (s32[]{:T(128)}, f32[128,1,5,128]{0,3,2,1:T(8,128)S(1)}, f32[4096,2,128]{2,0,1:T(8,128)}, s32[1,32]{1,0:T(1,128)S(1)}, s32[1,32]{1,0:T(1,128)S(1)}, ...) while((s32[]{:T(128)}, ...), condition=%wide.region_28.29_spmd.clone.clone, body=%wide.region_20.28_spmd.clone.clone.sunk | while | flops 423038848 | bytes 9862997 | solution.py:103
  526.8 6.5 conditional.18
  539.7 6.5 conditional.18
  565.1 38.9 %all-to-all-start.2 = ((bf16[32,128,2,128]{3,1,2,0:T(8,128)(2,1)}), bf16[32,128,2,128]{3,1,2,0:T(8,128)(2,1)}, u32[]{:S(2)}, u32[]{:S(2)}) async-start(bf16[32,128,2,128]{3,1,2,0:T(8,128)(2,1)} %copy.109), calls=%async_computation.2 | async-start | bytes 4194304 | tf_op jit(solution)/shard_map/all_to_all | solution.py:171
  609.0 85.5 %all-gather.23.cloned.1.call-done = bf16[4096,128]{1,0:T(8,128)(2,1)} async-done(((bf16[128,128]{1,0:T(8,128)(2,1)}), bf16[4096,128]{1,0:T(8,128)(2,1)}) %all-gather.23.cloned.1.call-update) | async-done | bytes 1048592 | tf_op jit(solution)/shard_map/all_gather | solution.py:166
  696.8 36.5 %while.87 = (s32[]{:T(128)}, f32[128,1,5,128]{0,3,2,1:T(8,128)S(1)}, f32[4096,2,128]{2,0,1:T(8,128)}, s32[1,32]{1,0:T(1,128)S(1)}, s32[1,32]{1,0:T(1,128)S(1)}, ...) while((s32[]{:T(128)}, ...), condition=%wide.region_37.38_spmd.clone.clone, body=%wide.region_29.37_spmd.clone.clone.sunk | while | flops 423038848 | bytes 9862997 | solution.py:103
  698.9 6.5 conditional.19
  711.8 6.5 conditional.19
  737.2 38.9 %all-to-all-start.3 = ((bf16[32,128,2,128]{3,1,2,0:T(8,128)(2,1)}), bf16[32,128,2,128]{3,1,2,0:T(8,128)(2,1)}, u32[]{:S(2)}, u32[]{:S(2)}) async-start(bf16[32,128,2,128]{3,1,2,0:T(8,128)(2,1)} %copy.110), calls=%async_computation.3 | async-start | bytes 4194304 | tf_op jit(solution)/shard_map/all_to_all | solution.py:171
  784.3 35.0 %all-to-all-done.3 = bf16[32,128,2,128]{3,1,2,0:T(8,128)(2,1)} async-done(((bf16[32,128,2,128]{3,1,2,0:T(8,128)(2,1)}), bf16[32,128,2,128]{3,1,2,0:T(8,128)(2,1)}, u32[]{:S(2)}, u32[]{:S(2)}) %all-to-all-start.3) | async-done | bytes 2097184 | tf_op jit(solution)/shard_map/all_to_all | solution.py:171
  821.3 24.2 %all-reduce = f32[1024]{0:T(1024)S(1)} all-reduce(f32[1024]{0:T(1024)S(1)} %pad_maximum_fusion.3), channel_id=2, replica_groups=mesh['dp'=16,'ctx'=32] {'dp'}, use_global_device_ids=true, to_apply=%region_45.46.clone | all-reduce | flops 1024 | bytes 8192
  845.6 73.0 %psum.8 = f32[64]{0:T(128)} all-reduce(f32[64]{0:T(128)S(1)} %dynamic-slice.1), channel_id=1, replica_groups=mesh['dp'=16,'ctx'=32] {'ctx'}, use_global_device_ids=true, to_apply=%region_44.45 | all-reduce | flops 64 | bytes 512 | tf_op jit(solution)/shard_map/psum | solution.py:183
  (423 shorter events, 208.9 us)
Async XLA Ops:
  7.2 8.5 copy-start.6
  7.2 87.7 %all-gather.11.cloned.1.call-start = ((), (), s32[]{:S(2)}) async-start(), calls=%async_computation.5 | async-start | bytes 1081344 | tf_op jit(solution)/shard_map/all_gather | solution.py:166
  8.8 169.3 %all-gather.9.cloned.1.call-start = ((), (), s32[]{:S(2)}) async-start(), calls=%async_computation.4 | async-start | bytes 1081344 | tf_op jit(solution)/shard_map/all_gather | solution.py:165
  10.3 254.1 %all-gather.13.cloned.1.call-start = ((), (), s32[]{:S(2)}) async-start(), calls=%async_computation.6 | async-start | bytes 1081344 | tf_op jit(solution)/shard_map/all_gather | solution.py:165
  11.0 338.7 %all-gather.15.cloned.1.call-start = ((), (), s32[]{:S(2)}) async-start(), calls=%async_computation.7 | async-start | bytes 1081344 | tf_op jit(solution)/shard_map/all_gather | solution.py:166
  11.6 421.2 %all-gather.17.cloned.1.call-start = ((), (), s32[]{:S(2)}) async-start(), calls=%async_computation.8 | async-start | bytes 1081344 | tf_op jit(solution)/shard_map/all_gather | solution.py:165
  12.2 510.3 %all-gather.19.cloned.1.call-start = ((), (), s32[]{:S(2)}) async-start(), calls=%async_computation.9 | async-start | bytes 1081344 | tf_op jit(solution)/shard_map/all_gather | solution.py:166
  12.8 596.2 %all-gather.21.cloned.1.call-start = ((), (), s32[]{:S(2)}) async-start(), calls=%async_computation.10 | async-start | bytes 1081344 | tf_op jit(solution)/shard_map/all_gather | solution.py:165
  13.5 681.0 %all-gather.23.cloned.1.call-start = ((), (), s32[]{:S(2)}) async-start(), calls=%async_computation.11 | async-start | bytes 1081344 | tf_op jit(solution)/shard_map/all_gather | solution.py:166
  16.0 0.7 copy-start.9
  16.0 1.1 copy-start.7
  17.1 0.7 copy-start.5
  178.1 2.2 copy-start.8
  220.9 171.6 %all-to-all-start = ((bf16[32,128,2,128]{3,1,2,0:T(8,128)(2,1)}), bf16[32,128,2,128]{3,1,2,0:T(8,128)(2,1)S(1)}, u32[]{:S(2)}, u32[]{:S(2)}) async-start(bf16[32,128,2,128]{3,1,2,0:T(8,128)(2,1)} %copy.107), calls=%async_computation | async-start | bytes 4194304 | tf_op jit(solution)/shard_map/all_to_all | solution.py:171
  349.7 2.2 copy-start.4
  392.5 1.3 copy-start
  393.8 171.3 %all-to-all-start.1 = ((bf16[32,128,2,128]{3,1,2,0:T(8,128)(2,1)}), bf16[32,128,2,128]{3,1,2,0:T(8,128)(2,1)}, u32[]{:S(2)}, u32[]{:S(2)}) async-start(bf16[32,128,2,128]{3,1,2,0:T(8,128)(2,1)} %copy.108), calls=%async_computation.1 | async-start | bytes 4194304 | tf_op jit(solution)/shard_map/all_to_all | solution.py:171
  522.5 2.2 copy-start.3
  565.1 172.1 %all-to-all-start.2 = ((bf16[32,128,2,128]{3,1,2,0:T(8,128)(2,1)}), bf16[32,128,2,128]{3,1,2,0:T(8,128)(2,1)}, u32[]{:S(2)}, u32[]{:S(2)}) async-start(bf16[32,128,2,128]{3,1,2,0:T(8,128)(2,1)} %copy.109), calls=%async_computation.2 | async-start | bytes 4194304 | tf_op jit(solution)/shard_map/all_to_all | solution.py:171
  694.5 2.2 copy-start.2
  737.2 82.1 %all-to-all-start.3 = ((bf16[32,128,2,128]{3,1,2,0:T(8,128)(2,1)}), bf16[32,128,2,128]{3,1,2,0:T(8,128)(2,1)}, u32[]{:S(2)}, u32[]{:S(2)}) async-start(bf16[32,128,2,128]{3,1,2,0:T(8,128)(2,1)} %copy.110), calls=%async_computation.3 | async-start | bytes 4194304 | tf_op jit(solution)/shard_map/all_to_all | solution.py:171
  778.2 1.8 copy-start.1
Sparse Core Ops, SparseCore 0:
  11.2 83.6 all-gather.10
  98.6 79.4 all-gather.8
  181.3 83.0 all-gather.12
  267.4 82.3 all-gather.14
  352.7 79.7 all-gather.16
  435.5 86.8 all-gather.18
  526.2 82.7 all-gather.20
  612.1 82.3 all-gather.22
where the time goes:
time: 932 us; the launch traced here: 927 us
  waiting for transfers between devices  466 us (50%)
  starting transfers between devices  156 us (17%)
  blocking collectives  97.2 us (10%)
  other arithmetic  86.9 us (9%)
  matrix products  53.8 us (6%)
  local copies, waits for them, and re-layouts  28.5 us (3%)
  loops' own time  23.4 us (3%)
  between operations  15.1 us (2%)
    all_gather x4, waiting for transfers between devices, on_device(): lax.all_gather(value_slice, 'ctx', axis=0, tiled=True)  335 us
    all_to_all x4, starting transfers between devices, on_device(): lax.all_to_all(shares, 'ctx', split_axis=0, concat_axis=0, tiled=True)  156 us
    all_gather x4, waiting for transfers between devices, on_device(): lax.all_gather(key_slice, 'ctx', axis=0, tiled=True)  92.7 us
    psum x1, blocking collectives, on_device(): across = lax.psum(column_sums, 'ctx')  73 us
    reduce_or x32, other arithmetic, one_tile(): return lax.cond(jnp.any(allowed), compute, unchanged, state)  38.3 us
    all_to_all x4, waiting for transfers between devices, on_device(): lax.all_to_all(shares, 'ctx', split_axis=0, concat_axis=0, tiled=True)  35 us
    unnamed x1, blocking collectives  24.2 us
    dynamic_update_slice x12, other arithmetic, compute(): lax.dynamic_update_slice_in_dim(key_value, current + update, offset, 0)  23.3 us
  transfers between devices with their start and end apart: 12, of which 8 were waited for; matrix products, arithmetic and copies ran while one was open for 17% of the time, Pallas kernels for 0%

commit v1 on v0

v1 whole, which is shorter than its diff:
```python
import functools

import jax
import jax.numpy as jnp
from jax import lax
from jax.experimental import pallas as pl
from jax.experimental.pallas import tpu as pltpu
from jax.sharding import PartitionSpec as P

KV = 4
GROUP = 5
D = 128
BLK = 128
ROWS = 8
COLS = 4
NB = ROWS * COLS
DP = 16
GW = GROUP * D
SCALE = D**-0.5
LOG2E = 1.4426950408889634
MESH = pl.DeviceIdType.MESH
ANY = pl.BlockSpec(memory_space=pl.ANY)
VMEM = pl.BlockSpec(memory_space=pltpu.VMEM)
SMEM = pl.BlockSpec(memory_space=pltpu.SMEM)
NT = (((1,), (1,)), ((), ()))
TN = (((0,), (0,)), ((), ()))


def dot(a, b, dims=(((1,), (0,)), ((), ()))):
    return lax.dot_general(a, b, dims, preferred_element_type=jnp.float32)


def place():
    c = lax.axis_index("ctx")
    return lax.axis_index("dp"), c // COLS, c % COLS


def cols(start, size):
    return pl.ds(pl.multiple_of(start, 128), size)


def greet(targets):
    barrier = pltpu.get_barrier_semaphore()
    for target in targets:
        pl.semaphore_signal(barrier, inc=1, device_id=target, device_id_type=MESH)
    pl.semaphore_wait(barrier, len(targets))


def send(src, dst, send_sem, recv_sem, target):
    copy = pltpu.make_async_remote_copy(
        src_ref=src,
        dst_ref=dst,
        send_sem=send_sem,
        recv_sem=recv_sem,
        device_id=target,
        device_id_type=MESH,
    )
    copy.start()
    return copy


def gather_kernel(
    q, do, o, k, v, lse,
    qh, doh, kall, vall, stat,
    do_v, o_v, lse_v, stat_v,
    own_sem, load_sem, kv_s, kv_r, q_s, q_r, st_s, st_r, up_s, up_r, dn_s, dn_r,
):
    dp, y, x = place()
    peers = [(x + j) % COLS for j in range(1, COLS)]
    above = (dp, ((y + 1) % ROWS) * COLS + x)
    below = (dp, ((y + ROWS - 1) % ROWS) * COLS + x)
    loads = [
        pltpu.make_async_copy(do, do_v, load_sem.at[0]),
        pltpu.make_async_copy(o, o_v, load_sem.at[1]),
        pltpu.make_async_copy(lse, lse_v, load_sem.at[2]),
    ]
    for c in loads:
        c.start()
    greet([(dp, y * COLS + p) for p in peers] + [above, below])
    kv = []
    for j, p in enumerate(peers):
        to = (dp, y * COLS + p)
        for n, (src, dst) in enumerate(((k, kall), (v, vall))):
            kv.append(
                send(src.at[:, cols(p * D, D)], dst.at[y, x], kv_s.at[j, n], kv_r.at[j, n], to)
            )
    own = [
        pltpu.make_async_copy(k.at[:, cols(x * D, D)], kall.at[y, x], own_sem.at[0]),
        pltpu.make_async_copy(v.at[:, cols(x * D, D)], vall.at[y, x], own_sem.at[1]),
        pltpu.make_async_copy(q.at[:, cols(x * GW, GW)], qh.at[x], own_sem.at[2]),
        pltpu.make_async_copy(do.at[:, cols(x * GW, GW)], doh.at[x], own_sem.at[3]),
    ]
    for c in own:
        c.start()
    big = []
    for j, p in enumerate(peers):
        to = (dp, y * COLS + p)
        for n, (src, dst) in enumerate(((q, qh), (do, doh))):
            big.append(
                send(src.at[:, cols(p * GW, GW)], dst.at[x], q_s.at[j, n], q_r.at[j, n], to)
            )
    own[0].wait()
    own[1].wait()
    for c in kv:
        c.wait_recv()

    def ring(step):
        out = []
        up_block = (y + ROWS - step) % ROWS
        dn_block = (y + step) % ROWS
        for n, full in ((0, kall), (1, vall)):
            if step < 3 or n == 0:
                out.append(send(full.at[up_block], full.at[up_block], up_s.at[step, n], up_r.at[step, n], above))
            if step < 3 or n == 1:
                out.append(send(full.at[dn_block], full.at[dn_block], dn_s.at[step, n], dn_r.at[step, n], below))
        return out

    flying = ring(0)
    for c in loads:
        c.wait()
    ones = jnp.ones((8, D), jnp.bfloat16)
    stat_v[...] = jnp.zeros_like(stat_v)
    for h in range(KV * GROUP):
        g, i = divmod(h, GROUP)
        prod = do_v[:, h * D : (h + 1) * D].astype(jnp.float32) * o_v[
            :, h * D : (h + 1) * D
        ].astype(jnp.float32)
        hi = prod.astype(jnp.bfloat16)
        rest = prod - hi.astype(jnp.float32)
        mid = rest.astype(jnp.bfloat16)
        total = dot(ones, hi, NT) + dot(ones, mid, NT)
        stat_v[g, 8 + i : 9 + i, :] = total[0:1]
        stat_v[g, i : i + 1, :] = lse_v[h : h + 1, :] * LOG2E
    stats = []
    for j, p in enumerate(peers):
        stats.append(
            send(stat_v.at[p], stat.at[x], st_s.at[j], st_r.at[j], (dp, y * COLS + p))
        )
    mine = pltpu.make_async_copy(stat_v.at[x], stat.at[x], own_sem.at[4])
    mine.start()
    for step in range(1, 4):
        for c in flying:
            c.wait_recv()
        for c in flying:
            c.wait_send()
        flying = ring(step)
    for c in flying:
        c.wait()
    for c in kv:
        c.wait_send()
    for c in big + stats:
        c.wait()
    own[2].wait()
    own[3].wait()
    mine.wait()


def gather(q, do, o, k, v, lse):
    bf = jnp.bfloat16
    sem = pltpu.SemaphoreType.DMA
    return pl.pallas_call(
        gather_kernel,
        out_shape=(
            jax.ShapeDtypeStruct((COLS, BLK, GW), bf),
            jax.ShapeDtypeStruct((COLS, BLK, GW), bf),
            jax.ShapeDtypeStruct((ROWS, COLS, BLK, D), bf),
            jax.ShapeDtypeStruct((ROWS, COLS, BLK, D), bf),
            jax.ShapeDtypeStruct((COLS, 16, BLK), jnp.float32),
        ),
        in_specs=[ANY] * 6,
        out_specs=[ANY] * 5,
        scratch_shapes=[
            pltpu.VMEM((BLK, KV * GW), bf),
            pltpu.VMEM((BLK, KV * GW), bf),
            pltpu.VMEM((KV * GROUP, BLK), jnp.float32),
            pltpu.VMEM((COLS, 16, BLK), jnp.float32),
            sem((5,)), sem((3,)), sem((3, 2)), sem((3, 2)), sem((3, 2)), sem((3, 2)),
            sem((3,)), sem((3,)), sem((4, 2)), sem((4, 2)), sem((4, 2)), sem((4, 2)),
        ],
        compiler_params=pltpu.CompilerParams(
            collective_id=0, has_side_effects=True, vmem_limit_bytes=16 << 20
        ),
        name="gather",
    )(q, do, o, k, v, lse)


def attend_kernel(path, live, qh, doh, kall, vall, stat, dqh, part, bias, dk, dv, dqt):
    c = lax.axis_index("ctx")
    y = c // COLS
    rows = 256
    dk[...] = jnp.zeros_like(dk)
    dv[...] = jnp.zeros_like(dv)
    nopen = jnp.where(path[0, 1] == 0, 2, 1)
    key_row = lax.broadcasted_iota(jnp.int32, (rows, GW), 0)

    def pieces(i, kc, vc, keep):
        qi, gi = qh[i], doh[i]
        heads = lambda a: jnp.concatenate([a[:, n * D : (n + 1) * D] for n in range(GROUP)], axis=0)
        qs, gs = heads(qi), heads(gi)
        flat = lambda first: jnp.concatenate(
            [stat[i, first + n : first + n + 1, :] for n in range(GROUP)], axis=1
        )
        s = dot(kc, qs, NT)
        p = jnp.where(keep, jnp.exp2(s * (SCALE * LOG2E) - flat(0)), 0.0)
        t = dot(vc, gs, NT)
        ds = (p * (t - flat(8))).astype(jnp.bfloat16)
        return dot(ds, qs), dot(p.astype(jnp.bfloat16), gs), dot(kc, ds, TN)

    for i in range(COLS):
        b = y * COLS + i
        mine = path[0, b]
        at = pl.ds(pl.multiple_of(b * BLK, BLK), BLK)
        query_col = lax.broadcasted_iota(jnp.int32, (BLK, GW), 1) % BLK
        row = lax.broadcasted_iota(jnp.int32, (BLK, GW), 0)
        keep = (row <= query_col) & (row < live[0, b])
        a, v_part, q_part = pieces(i, kall[at, :], vall[at, :], keep)
        dk[at, :] += a
        dv[at, :] += v_part
        dqt[...] = q_part
        start = lax.while_loop(
            lambda r: (r > 0) & (path[0, jnp.maximum(r - 1, 0)] == mine), lambda r: r - 1, b
        )
        shared = mine == 0
        first_end = jnp.where(shared, 0, nopen)
        start = jnp.where(shared, 0, start)

        def span(lower, upper):
            def step(n, _):
                kb = lower + 2 * n
                two = pl.ds(pl.multiple_of(kb * BLK, BLK), rows)
                second = jnp.where(kb + 1 < upper, live[0, jnp.minimum(kb + 1, NB - 1)], 0)
                keep = key_row < jnp.where(key_row < BLK, live[0, kb], BLK + second)
                a, v_part, q_part = pieces(i, kall[two, :], vall[two, :], keep)
                dk[two, :] += a
                dv[two, :] += v_part
                dqt[...] += q_part
                return 0

            lax.fori_loop(0, (upper - lower + 1) // 2, step, 0)

        span(0, first_end)
        span(start, b)
        for n in range(GROUP):
            dqh[i, :, n * D : (n + 1) * D] = (
                dqt[:, n * D : (n + 1) * D] * SCALE
            ).T.astype(jnp.bfloat16)

    bias[...] = jnp.zeros_like(bias)

    def finish(n, sums):
        at = pl.ds(pl.multiple_of(n * 512, 512), 512)
        a = dk[at, :] * SCALE
        b = dv[at, :]
        part[n, 0] = a.astype(jnp.bfloat16)
        part[n, 1] = b.astype(jnp.bfloat16)
        return (
            sums[0] + jnp.sum(a, axis=0, keepdims=True),
            sums[1] + jnp.sum(b, axis=0, keepdims=True),
        )

    zero = jnp.zeros((1, D), jnp.float32)
    ka, va = lax.fori_loop(0, ROWS, finish, (zero, zero))
    bias[0:1, :] = ka
    bias[1:2, :] = va


def attend(path, live, qh, doh, kall, vall, stat):
    bf = jnp.bfloat16
    return pl.pallas_call(
        attend_kernel,
        out_shape=(
            jax.ShapeDtypeStruct((COLS, BLK, GW), bf),
            jax.ShapeDtypeStruct((ROWS, 2, COLS * BLK, D), bf),
            jax.ShapeDtypeStruct((8, D), jnp.float32),
        ),
        in_specs=[SMEM, SMEM] + [VMEM] * 5,
        out_specs=[VMEM] * 3,
        scratch_shapes=[
            pltpu.VMEM((NB * BLK, D), jnp.float32),
            pltpu.VMEM((NB * BLK, D), jnp.float32),
            pltpu.VMEM((BLK, GW), jnp.float32),
        ],
        compiler_params=pltpu.CompilerParams(vmem_limit_bytes=40 << 20),
        name="attend",
    )(path, live, qh, doh, kall.reshape(NB * BLK, D), vall.reshape(NB * BLK, D), stat)


def give_back_kernel(
    dqh, part, biasp,
    dq, dkv_k, dkv_v, bias,
    down, up, down_out, up_out, final, by, bd, bx,
    own_sem, q_s, q_r, dn_s, dn_r, up_s, up_r, f_s, f_r, y_s, y_r, d_s, d_r, x_s, x_r,
):
    dp, y, x = place()
    c = y * COLS + x
    peers = [(x + j) % COLS for j in range(1, COLS)]
    above = (dp, ((y + 1) % ROWS) * COLS + x)
    below = (dp, ((y + ROWS - 1) % ROWS) * COLS + x)
    in_row = [(dp, y * COLS + p) for p in peers]
    in_col = [(dp, ((y + j) % ROWS) * COLS + x) for j in range(1, ROWS)]
    in_dp = [((dp + j) % DP, c) for j in range(1, DP)]
    greet(in_row + in_col + in_dp)

    def ring(step):
        out = []
        owner_dn = (y + ROWS - 4 + step) % ROWS
        owner_up = (y + 4 - step) % ROWS
        for n in (0, 1):
            for way, owner, land, stage, ss, rs, to, first in (
                (0, owner_dn, down, down_out, dn_s, dn_r, below, n),
                (1, owner_up, up, up_out, up_s, up_r, above, 1 - n),
            ):
                if step < first:
                    continue
                if step == first:
                    src = part.at[owner, n]
                else:
                    before[way, n].wait_recv()
                    stage[step, n] = (
                        land[step - 1, n].astype(jnp.float32)
                        + part[owner, n].astype(jnp.float32)
                    ).astype(jnp.bfloat16)
                    src = stage.at[step, n]
                copy = send(src, land.at[step, n], ss.at[step, n], rs.at[step, n], to)
                before[way, n] = copy
                out.append(copy)
        return out

    before = {}
    started = ring(0)
    by[y] = biasp[...]
    col = [send(by.at[y], by.at[y], y_s.at[j], y_r.at[j], t) for j, t in enumerate(in_col)]
    own_q = pltpu.make_async_copy(dqh.at[x], dq.at[:, cols(x * GW, GW)], own_sem.at[0])
    own_q.start()
    back = [
        send(dqh.at[p], dq.at[:, cols(x * GW, GW)], q_s.at[j], q_r.at[j], in_row[j])
        for j, p in enumerate(peers)
    ]
    started += ring(1)
    for copy in col:
        copy.wait()
    bd[dp] = jnp.sum(by[...], axis=0)
    deep = [send(bd.at[dp], bd.at[dp], d_s.at[j], d_r.at[j], t) for j, t in enumerate(in_dp)]
    started += ring(2)
    for copy in deep:
        copy.wait()
    bx[x] = jnp.sum(bd[...], axis=0)
    wide = [send(bx.at[x], bx.at[x], x_s.at[j], x_r.at[j], t) for j, t in enumerate(in_row)]
    started += ring(3)
    for copy in wide:
        copy.wait()
    entry = bx[(dp % 8) // 2]
    picked = jnp.where(dp < 8, entry[0:1], entry[1:2])
    swapped = jnp.concatenate([picked[:, 64:], picked[:, :64]], axis=1)
    bias[...] = jnp.where(dp % 2 == 0, picked, swapped)
    last = []
    for n, dst in ((0, dkv_k), (1, dkv_v)):
        before[0, n].wait_recv()
        before[1, n].wait_recv()
        total = (
            part[y, n].astype(jnp.float32)
            + down[3, n].astype(jnp.float32)
            + up[3, n].astype(jnp.float32)
        )
        final[n] = total.astype(jnp.bfloat16).reshape(COLS, BLK, D)
        for j, p in enumerate(peers):
            last.append(
                send(final.at[n, p], dst.at[:, cols(x * D, D)], f_s.at[j, n], f_r.at[j, n], in_row[j])
            )
        last_own = pltpu.make_async_copy(
            final.at[n, x], dst.at[:, cols(x * D, D)], own_sem.at[1 + n]
        )
        last_own.start()
        last.append(last_own)
    for copy in started:
        copy.wait_send()
    for copy in back:
        copy.wait()
    own_q.wait()
    for copy in last:
        copy.wait()


def give_back(dqh, part, biasp):
    bf = jnp.bfloat16
    sem = pltpu.SemaphoreType.DMA
    land = pltpu.VMEM((4, 2, COLS * BLK, D), bf)
    return pl.pallas_call(
        give_back_kernel,
        out_shape=(
            jax.ShapeDtypeStruct((BLK, KV * GW), bf),
            jax.ShapeDtypeStruct((BLK, KV * D), bf),
            jax.ShapeDtypeStruct((BLK, KV * D), bf),
            jax.ShapeDtypeStruct((1, D), jnp.float32),
        ),
        in_specs=[ANY, VMEM, VMEM],
        out_specs=[ANY, ANY, ANY, VMEM],
        scratch_shapes=[
            land, land, land, land,
            pltpu.VMEM((2, COLS, BLK, D), bf),
            pltpu.VMEM((ROWS, 8, D), jnp.float32),
            pltpu.VMEM((DP, 8, D), jnp.float32),
            pltpu.VMEM((COLS, 8, D), jnp.float32),
            sem((3,)), sem((3,)), sem((3,)),
            sem((4, 2)), sem((4, 2)), sem((4, 2)), sem((4, 2)),
            sem((3, 2)), sem((3, 2)),
            sem((7,)), sem((7,)), sem((15,)), sem((15,)), sem((3,)), sem((3,)),
        ],
        compiler_params=pltpu.CompilerParams(
            collective_id=1, has_side_effects=True, vmem_limit_bytes=32 << 20
        ),
        name="give_back",
    )(dqh, part, biasp)


def on_device(queries, keys, values, outputs, d_out, log_sums, block_path, live_len):
    qh, doh, kall, vall, stat = gather(
        queries[0], d_out[0], outputs[0], keys[0], values[0], log_sums[0]
    )
    dqh, part, biasp = attend(block_path, live_len, qh, doh, kall, vall, stat)
    dq, dk, dv, bias = give_back(dqh, part, biasp)
    return dq[None], dk[None], dv[None], bias[0, :64]


def solution(mesh):
    wide = P("dp", "ctx", None)
    return jax.shard_map(
        on_device,
        mesh=mesh,
        in_specs=(wide, wide, wide, wide, wide, P("dp", None, "ctx"), P("dp", None), P("dp", None)),
        out_specs=(wide, wide, wide, P("dp")),
        check_vma=False,
    )
```

time: 932 us -> 122 us (0.13)
  the two profiles are of different devices: /device:TPU:32 before, /device:TPU:2 now
where the time goes in v1:
time: 122 us; the launch traced here: 121 us
  Pallas kernels  112 us (92%)
  local copies, waits for them, and re-layouts  8.45 us (7%)
    pallas_call x1, Pallas kernels, give_back(): pl.pallas_call(give_back_kernel, out_shape=(jax.ShapeDtypeStruct((BLK, KV...  63.4 us
    pallas_call x1, Pallas kernels, gather(): pl.pallas_call(gather_kernel, out_shape=(jax.ShapeDtypeStruct((COLS, BLK,...  41.6 us
    unnamed x18, local copies, waits for them, and re-layouts  7.94 us
    pallas_call x1, Pallas kernels, attend(): pl.pallas_call(attend_kernel, out_shape=(jax.ShapeDtypeStruct((COLS, BLK,...  7.03 us

profile of v1, /device:TPU:2, one launch (start us, length us, event | category | flops | bytes accessed | tf_op | source)
XLA Modules:
  0.0 121.1 jit_solution(1958516460324376734)
XLA Ops:
  0.6 0.0 copy-start.6
  0.6 0.0 copy-start.5
  0.7 0.7 copy.14
  1.4 0.0 copy-start
  1.4 1.1 copy-done
  2.5 0.0 copy-start.1
  2.5 1.1 copy-done.1
  3.5 0.0 copy-start.2
  3.5 1.1 copy-done.2
  4.6 0.0 copy-start.3
  4.6 0.9 copy-done.3
  5.5 0.0 copy-start.4
  5.5 0.9 copy-done.4
  6.4 41.6 %gather.1 = (bf16[4,128,640]{2,1,0:T(8,128)(2,1)S(1)}, bf16[4,128,640]{2,1,0:T(8,128)(2,1)S(1)}, bf16[8,4,128,128]{3,2,1,0:T(8,128)(2,1)S(1)}, bf16[8,4,128,128]{3,2,1,0:T(8,128)(2,1)S(1)}, f32[4,16,128]{2,1,0:T(8,128)S(1)}) custom-call(bf16[128,2560]{1,0:T(8,128)(2,1)S(1)} %bitcast.18, bf16[128,2560]{1,0:T(8,128)(2,1)S(1)} %bitcast.19, ...), custom_call_target="tpu_custom_call" | custom-call | tf_op jit(solution)/shard_map/gather/pallas_call | solution.py:161
  48.0 0.0 copy-done.6
  48.0 0.0 copy-done.5
  48.0 7.0 %attend.1 = (bf16[4,128,640]{2,1,0:T(8,128)(2,1)S(1)}, bf16[8,2,512,128]{3,2,1,0:T(8,128)(2,1)S(1)}, f32[8,128]{1,0:T(8,128)S(1)}) custom-call(s32[1,32]{1,0:T(1,128)S(1)} %copy-done.5, s32[1,32]{1,0:T(1,128)S(1)} %copy-done.6, bf16[4,128,640]{2,1,0:T(8,128)(2,1)S(1)} %get-tuple-element.16.qh, bf16[4,128,640]{2,1,0:T(8,128)(2,1)S(1)} %get-tuple-element.17.doh, ...), custom_call_target="tpu_custom_call" | custom-call | tf_op jit(solution)/shard_map/attend/pallas_call | solution.py:269
  55.1 63.4 %give_back.1 = (bf16[128,2560]{1,0:T(8,128)(2,1)S(1)}, bf16[128,512]{1,0:T(8,128)(2,1)S(1)}, bf16[128,512]{1,0:T(8,128)(2,1)S(1)}, f32[1,128]{1,0:T(1,128)S(1)}) custom-call(bf16[4,128,640]{2,1,0:T(8,128)(2,1)S(1)} %get-tuple-element.21.dqh, bf16[8,2,512,128]{3,2,1,0:T(8,128)(2,1)S(1)} %get-tuple-element.22.part, f32[8,128]{1,0:T(8,128)S(1)} %get-tuple-element.23.biasp), custom_call_target="tpu_custom_call" | custom-call | tf_op jit(solution)/shard_map/give_back/pallas_call | solution.py:388
  118.5 0.5 slice_bitcast_fusion
  119.0 0.8 copy.18
  119.8 0.7 copy.19
  120.5 0.7 copy.20
Async XLA Ops:
  0.6 47.4 %copy-start.6 = (s32[1,32]{1,0:T(1,128)S(1)}, s32[1,32]{1,0:T(1,128)}, u32[]{:S(2)}) copy-start(s32[1,32]{1,0:T(1,128)} %live.1) | copy-start | bytes 388
  0.6 47.4 %copy-start.5 = (s32[1,32]{1,0:T(1,128)S(1)}, s32[1,32]{1,0:T(1,128)}, u32[]{:S(2)}) copy-start(s32[1,32]{1,0:T(1,128)} %path.1) | copy-start | bytes 388
  1.4 1.1 copy-start
  2.5 1.1 copy-start.1
  3.5 1.1 copy-start.2
  4.6 0.9 copy-start.3
  5.5 0.9 copy-start.4

commit v2 on v1

v2 whole, which is shorter than its diff:
```python
import functools

import jax
import jax.numpy as jnp
from jax import lax
from jax.experimental import pallas as pl
from jax.experimental.pallas import tpu as pltpu
from jax.sharding import PartitionSpec as P

KV = 4
GROUP = 5
D = 128
BLK = 128
ROWS = 8
COLS = 4
NB = ROWS * COLS
DP = 16
GW = GROUP * D
SCALE = D**-0.5
LOG2E = 1.4426950408889634
FAR = 1e30
FAR_ROWS = ROWS - 3
LIMIT = 60 << 20
MESH = pl.DeviceIdType.MESH
ANY = pl.BlockSpec(memory_space=pl.ANY)
VMEM = pl.BlockSpec(memory_space=pltpu.VMEM)
SMEM = pl.BlockSpec(memory_space=pltpu.SMEM)
NT = (((1,), (1,)), ((), ()))
TN = (((0,), (0,)), ((), ()))


def dot(a, b, dims=(((1,), (0,)), ((), ()))):
    return lax.dot_general(a, b, dims, preferred_element_type=jnp.float32)


def place():
    c = lax.axis_index("ctx")
    return lax.axis_index("dp"), c // COLS, c % COLS


def cols(start, size):
    return pl.ds(pl.multiple_of(start, 128), size)


def greet(targets):
    barrier = pltpu.get_barrier_semaphore()
    for target in targets:
        pl.semaphore_signal(barrier, inc=1, device_id=target, device_id_type=MESH)
    pl.semaphore_wait(barrier, len(targets))


def send(src, dst, send_sem, recv_sem, target):
    copy = pltpu.make_async_remote_copy(
        src_ref=src,
        dst_ref=dst,
        send_sem=send_sem,
        recv_sem=recv_sem,
        device_id=target,
        device_id_type=MESH,
    )
    copy.start()
    return copy


def unit(i, b, row, x, path, kc, vc, qref, gref, stat, dk_at, dv_at, dqt):
    heads = lambda a: jnp.concatenate([a[:, n * D : (n + 1) * D] for n in range(GROUP)], axis=0)
    flat = lambda first: jnp.concatenate(
        [stat[i, first + n : first + n + 1, :] for n in range(GROUP)], axis=1
    )
    qs, gs = heads(qref[i]), heads(gref[i])
    base, delta = flat(0), flat(8)
    mine = path[0, b]
    s = dot(kc, qs, NT)
    t = dot(vc, gs, NT)
    behind = lax.broadcasted_iota(jnp.int32, (BLK, GW), 0) - (
        lax.broadcasted_iota(jnp.int32, (BLK, GW), 1) % BLK
    )
    p_low, ds = [], []
    for j in range(COLS):
        kb = row * COLS + (x + j) % COLS
        theirs = path[0, kb]
        joined = (theirs == 0) | (theirs == mine) | (mine == 0)
        shift = base + jnp.where(joined, 0.0, FAR)
        at = slice(j * BLK, (j + 1) * BLK)
        p = jnp.exp2(s[at] * (SCALE * LOG2E) - shift)
        p = jnp.where(behind <= BLK * (b - kb), p, 0.0)
        p_low.append(p.astype(jnp.bfloat16))
        ds.append((p * (t[at] - delta)).astype(jnp.bfloat16))
    p_low = jnp.concatenate(p_low, axis=0)
    ds = jnp.concatenate(ds, axis=0)
    dk_at[...] += dot(ds, qs)
    dv_at[...] += dot(p_low, gs)
    dqt[i] += dot(kc, ds, TN)


def close_row(row, x, live, dk_at, dv_at, part_at, sums):
    key_row = lax.broadcasted_iota(jnp.int32, (BLK, D), 0)
    ka, va = sums
    for j in range(COLS):
        at = slice(j * BLK, (j + 1) * BLK)
        keep = key_row < live[0, row * COLS + (x + j) % COLS]
        a = jnp.where(keep, dk_at[at, :] * SCALE, 0.0)
        b = jnp.where(keep, dv_at[at, :], 0.0)
        part_at[0, at, :] = a.astype(jnp.bfloat16)
        part_at[1, at, :] = b.astype(jnp.bfloat16)
        ka += jnp.sum(a, axis=0, keepdims=True)
        va += jnp.sum(b, axis=0, keepdims=True)
    return ka, va


def no_sums():
    return jnp.zeros((1, D), jnp.float32), jnp.zeros((1, D), jnp.float32)


def gather_kernel(
    path, live, q, do, o, k, v, lse,
    qh, doh, stat, dqt_out, near_out, far, bias,
    do_v, o_v, lse_v, k_v, own_stat, q_v, g_v, kv_all, stat_v, dk, dv, dqt, near_v,
    own_sem, load_sem, out_sem, kv_s, kv_r, q_s, q_r, st_s, st_r, up_s, up_r, dn_s, dn_r,
):
    dp, y, x = place()
    c = y * COLS + x
    peers = [(x + j) % COLS for j in range(1, COLS)]
    above = (dp, ((y + 1) % ROWS) * COLS + x)
    below = (dp, ((y + ROWS - 1) % ROWS) * COLS + x)
    spot = lambda j: pl.ds(j * BLK, BLK)
    rest = pl.ds(BLK, 3 * BLK)
    loads = [
        pltpu.make_async_copy(k, k_v, load_sem.at[0]),
        pltpu.make_async_copy(do, do_v, load_sem.at[1]),
        pltpu.make_async_copy(o, o_v, load_sem.at[2]),
        pltpu.make_async_copy(lse, lse_v, load_sem.at[3]),
    ]
    for copy in loads:
        copy.start()
    own_q = [
        pltpu.make_async_copy(q.at[:, cols(x * GW, GW)], q_v.at[x], own_sem.at[2]),
        pltpu.make_async_copy(do.at[:, cols(x * GW, GW)], g_v.at[x], own_sem.at[3]),
    ]
    own_v = pltpu.make_async_copy(v.at[:, cols(x * D, D)], kv_all.at[y, 1, spot(0)], own_sem.at[1])
    for copy in own_q + [own_v]:
        copy.start()
    greet([(dp, y * COLS + p) for p in peers] + [above, below])
    kv, big = {}, {}
    for j, p in enumerate(peers):
        kv[j, 1] = send(
            v.at[:, cols(p * D, D)], kv_all.at[y, 1, spot(3 - j)], kv_s.at[j, 1], kv_r.at[j, 1],
            (dp, y * COLS + p),
        )
    loads[0].wait()
    key_row = lax.broadcasted_iota(jnp.int32, (BLK, KV * D), 0)
    k_v[...] = jnp.where(key_row < live[0, c], k_v[...].astype(jnp.float32), 0.0).astype(
        jnp.bfloat16
    )
    for j, p in enumerate(peers):
        kv[j, 0] = send(
            k_v.at[:, cols(p * D, D)], kv_all.at[y, 0, spot(3 - j)], kv_s.at[j, 0], kv_r.at[j, 0],
            (dp, y * COLS + p),
        )
    own_k = pltpu.make_async_copy(k_v.at[:, cols(x * D, D)], kv_all.at[y, 0, spot(0)], own_sem.at[0])
    own_k.start()
    ring = {}

    def piece(block, n, part):
        full = kv_all.at[block]
        if part == 0:
            return full.at[:, spot(0)] if n is None else full.at[n, spot(0)]
        return full.at[part - 1, rest]

    def forward(step, part):
        up_block = (y + ROWS - step) % ROWS
        dn_block = (y + step) % ROWS
        half = None if step < 3 else 0
        if step:
            ring[step - 1, part, 0].wait_recv()
        if step < 3 or part != 2:
            at = piece(up_block, half, part)
            ring[step, part, 0] = send(
                at, at, up_s.at[step, part], up_r.at[step, part], above
            )
        if step:
            ring[step - 1, part, 1].wait_recv()
        if step < 3 or part != 1:
            at = piece(dn_block, None if step < 3 else 1, part)
            ring[step, part, 1] = send(
                at, at, dn_s.at[step, part], dn_r.at[step, part], below
            )

    own_v.wait()
    own_k.wait()
    forward(0, 0)
    for j in range(3):
        kv[j, 1].wait_recv()
    forward(0, 2)
    for j in range(3):
        kv[j, 0].wait_recv()
    forward(0, 1)

    def move(*which):
        for j in which:
            for n, (src, dst) in enumerate(((q, q_v), (do, g_v))):
                big[j, n] = send(
                    src.at[:, cols(peers[j] * GW, GW)], dst.at[x], q_s.at[j, n], q_r.at[j, n],
                    (dp, y * COLS + peers[j]),
                )

    move(0, 2)
    for copy in loads[1:]:
        copy.wait()
    ones = jnp.ones((8, D), jnp.bfloat16)
    own_stat[...] = jnp.zeros_like(own_stat)
    for h in range(KV * GROUP):
        g, i = divmod(h, GROUP)
        prod = do_v[:, h * D : (h + 1) * D].astype(jnp.float32) * o_v[
            :, h * D : (h + 1) * D
        ].astype(jnp.float32)
        hi = prod.astype(jnp.bfloat16)
        mid = (prod - hi.astype(jnp.float32)).astype(jnp.bfloat16)
        total = dot(ones, hi, NT) + dot(ones, mid, NT)
        own_stat[g, 8 + i : 9 + i, :] = total[0:1]
        own_stat[g, i : i + 1, :] = lse_v[h] * LOG2E
    stats = [
        send(own_stat.at[p], stat_v.at[x], st_s.at[j], st_r.at[j], (dp, y * COLS + p))
        for j, p in enumerate(peers)
    ]
    mine = pltpu.make_async_copy(own_stat.at[x], stat_v.at[x], own_sem.at[4])
    mine.start()
    dk[...] = jnp.zeros_like(dk)
    dv[...] = jnp.zeros_like(dv)
    dqt[...] = jnp.zeros_like(dqt)

    def pairs(i, row, slot, valid):
        @pl.when(valid)
        def _():
            unit(
                i % COLS, y * COLS + i % COLS, row, x, path, kv_all[row, 0], kv_all[row, 1],
                q_v, g_v, stat_v, dk.at[slot], dv.at[slot], dqt,
            )

    def own_pair(j):
        pairs(x + j, y, 0, y >= 0)

    def last_pair(j):
        pairs(x + j, jnp.maximum(y - 1, 0), 1, y >= 1)

    def back_pair(j):
        pairs(x + j, jnp.maximum(y - 2, 0), 2, y >= 2)

    def open_pair(j):
        pairs(x + j, 0, 3, y >= 6)

    mine.wait()
    for copy in own_q:
        copy.wait()
    forward(1, 0)
    own_pair(0)
    forward(1, 2)
    forward(1, 1)
    move(1)
    last_pair(0)
    for j in (0, 2):
        stats[j].wait_recv()
        big[j, 0].wait_recv()
        big[j, 1].wait_recv()
    forward(2, 0)
    own_pair(1)
    forward(2, 2)
    own_pair(3)
    forward(2, 1)
    last_pair(1)
    last_pair(3)
    back_pair(0)
    forward(3, 0)
    back_pair(1)
    back_pair(3)
    open_pair(0)
    forward(3, 2)
    open_pair(1)
    open_pair(3)
    forward(3, 1)
    stats[1].wait_recv()
    big[1, 0].wait_recv()
    big[1, 1].wait_recv()
    outs = [
        pltpu.make_async_copy(q_v, qh, out_sem.at[0]),
        pltpu.make_async_copy(g_v, doh, out_sem.at[1]),
        pltpu.make_async_copy(stat_v, stat, out_sem.at[2]),
    ]
    for copy in outs:
        copy.start()
    own_pair(2)
    last_pair(2)
    back_pair(2)
    open_pair(2)
    outs.append(pltpu.make_async_copy(dqt, dqt_out, out_sem.at[5]))
    outs[-1].start()
    sums = no_sums()
    for slot, row in enumerate((y, (y + ROWS - 1) % ROWS, (y + ROWS - 2) % ROWS, 0)):
        sums = close_row(row, x, live, dk.at[slot], dv.at[slot], near_v.at[slot], sums)
    outs.append(pltpu.make_async_copy(near_v, near_out, out_sem.at[6]))
    outs[-1].start()
    bias[...] = jnp.zeros_like(bias)
    bias[0:1, :] = sums[0]
    bias[1:2, :] = sums[1]
    for part, way in ((0, 0), (1, 0), (0, 1), (2, 1)):
        ring[3, part, way].wait_recv()
    ends = [pltpu.make_async_copy(kv_all.at[pl.ds(0, FAR_ROWS)], far, out_sem.at[8])]
    for copy in ends:
        copy.start()
    for copy in list(ring.values()) + list(kv.values()) + list(big.values()) + stats:
        copy.wait_send()
    for copy in outs + ends:
        copy.wait()


def gather(path, live, q, do, o, k, v, lse):
    bf = jnp.bfloat16
    f32 = jnp.float32
    sem = pltpu.SemaphoreType.DMA
    rows = COLS * BLK
    heads = ((COLS, BLK, GW), bf)
    whole = ((ROWS, 2, rows, D), bf)
    far = ((FAR_ROWS, 2, rows, D), bf)
    stat = ((COLS, 16, BLK), f32)
    dqt = ((COLS, BLK, GW), f32)
    near = ((4, 2, rows, D), bf)
    outs = [heads, heads, stat, dqt, near, far, ((8, D), f32)]
    full = ((BLK, KV * GW), bf)
    slots = ((4, rows, D), f32)
    scratch = [
        full, full, ((KV * GROUP, 1, BLK), f32), ((BLK, KV * D), bf), stat,
        heads, heads, whole, stat, slots, slots, dqt, near,
    ]
    return pl.pallas_call(
        gather_kernel,
        out_shape=tuple(jax.ShapeDtypeStruct(*s) for s in outs),
        in_specs=[SMEM, SMEM] + [ANY] * 6,
        out_specs=[ANY] * 6 + [VMEM],
        scratch_shapes=[pltpu.VMEM(*s) for s in scratch] + [
            sem((5,)), sem((4,)), sem((9,)), sem((3, 2)), sem((3, 2)), sem((3, 2)), sem((3, 2)),
            sem((3,)), sem((3,)), sem((4, 3)), sem((4, 3)), sem((4, 3)), sem((4, 3)),
        ],
        compiler_params=pltpu.CompilerParams(
            collective_id=0, has_side_effects=True, vmem_limit_bytes=LIMIT
        ),
        name="gather",
    )(path, live, q, do, o, k, v, lse)


def attend_kernel(
    path, live, qh, doh, stat, dqt_near, far, near, bias_near,
    part, dqh, bias,
    q_v, g_v, stat_v, far_v, part_v, dk, dv, dqt, dqh_v, sem, near_sem, out_sem,
):
    y = lax.axis_index("ctx") // COLS
    x = lax.axis_index("ctx") % COLS
    early = y >= 6
    lower = jnp.where(early, 1, 0)
    upper = jnp.maximum(y - 2, 0)
    some = upper > lower
    placed = (
        (0, y, y >= 0), (1, y - 1, y >= 1), (2, y - 2, y >= 2), (3, 0, early),
    )
    near_copy = lambda slot, row: pltpu.make_async_copy(
        near.at[slot], part_v.at[row], near_sem.at[slot]
    )
    loads = [
        pltpu.make_async_copy(src, dst, sem.at[n])
        for n, (src, dst) in enumerate(
            ((far, far_v), (qh, q_v), (stat, stat_v), (doh, g_v))
        )
    ]

    @pl.when(some)
    def _():
        for copy in loads:
            copy.start()

    for slot, row, valid in placed:

        @pl.when(valid)
        def _(slot=slot, row=row):
            near_copy(slot, row).start()

    def blank(n, _):
        part_v[n] = jnp.zeros((2, COLS * BLK, D), jnp.bfloat16)
        return 0

    lax.fori_loop(y + 1, ROWS, blank, 0)
    out_q = pltpu.make_async_copy(dqh_v, dqh, out_sem.at[0])
    load_q = pltpu.make_async_copy(dqt_near, dqt, sem.at[4])
    load_q.start()

    def clear(n, _):
        dk[n] = jnp.zeros((COLS * BLK, D), jnp.float32)
        dv[n] = jnp.zeros((COLS * BLK, D), jnp.float32)
        return 0

    lax.fori_loop(lower, upper, clear, 0)
    load_q.wait()

    @pl.when(some)
    def _():
        for copy in loads:
            copy.wait()

        def query(i, _):
            b = y * COLS + i
            mine = path[0, b]

            def one(row, _):
                seen = lambda kb: (path[0, kb] == 0) | (path[0, kb] == mine) | (mine == 0)
                kb = row * COLS
                needed = seen(kb) | seen(kb + 1) | seen(kb + 2) | seen(kb + 3)

                @pl.when(needed)
                def _():
                    unit(
                        i, b, row, x, path, far_v[row, 0], far_v[row, 1], q_v, g_v, stat_v,
                        dk.at[row], dv.at[row], dqt,
                    )

                return 0

            lax.fori_loop(lower, upper, one, 0)
            return 0

        lax.fori_loop(0, COLS, query, 0)

    def finish_query(i, _):
        for n in range(GROUP):
            at = slice(n * D, (n + 1) * D)
            dqh_v[i, :, at] = (dqt[i, :, at] * SCALE).T.astype(jnp.bfloat16)
        return 0

    lax.fori_loop(0, COLS, finish_query, 0)
    out_q.start()

    sums = lax.fori_loop(
        lower,
        upper,
        lambda n, s: close_row(n, x, live, dk.at[n], dv.at[n], part_v.at[n], s),
        (bias_near[0:1, :], bias_near[1:2, :]),
    )
    bias[...] = jnp.zeros_like(bias)
    bias[0:1, :] = sums[0]
    bias[1:2, :] = sums[1]
    for slot, row, valid in placed:

        @pl.when(valid)
        def _(slot=slot, row=row):
            near_copy(slot, row).wait()

    out_part = pltpu.make_async_copy(part_v, part, out_sem.at[1])
    out_part.start()
    out_part.wait()
    out_q.wait()


def attend(path, live, qh, doh, stat, dqt_near, far, near, bias_near):
    bf = jnp.bfloat16
    f32 = jnp.float32
    rows = COLS * BLK
    sem = pltpu.SemaphoreType.DMA
    heads = ((COLS, BLK, GW), bf)
    kept = ((FAR_ROWS, 2, rows, D), bf)
    part = ((ROWS, 2, rows, D), bf)
    dqt = ((COLS, BLK, GW), f32)
    grads = ((FAR_ROWS, rows, D), f32)
    scratch = [heads, heads, ((COLS, 16, BLK), f32), kept, part, grads, grads, dqt, heads]
    return pl.pallas_call(
        attend_kernel,
        out_shape=tuple(jax.ShapeDtypeStruct(*s) for s in (part, heads, ((8, D), f32))),
        in_specs=[SMEM, SMEM] + [ANY] * 6 + [VMEM],
        out_specs=[ANY, ANY, VMEM],
        scratch_shapes=[pltpu.VMEM(*s) for s in scratch] + [sem((5,)), sem((4,)), sem((2,))],
        compiler_params=pltpu.CompilerParams(vmem_limit_bytes=LIMIT),
        name="attend",
    )(path, live, qh, doh, stat, dqt_near, far, near, bias_near)


def flip(value, bit):
    return value + bit - 2 * bit * ((value // bit) % 2)


def give_back_kernel(
    part, biasp, dqh,
    dq, dkv_k, dkv_v, bias,
    part_v, down, up, down_out, up_out, final, totals, inbox, bx, bd,
    load_sem, own_sem, q_s, q_r, dn_s, dn_r, up_s, up_r, f_s, f_r, b_s, b_r, x_s, x_r, d_s, d_r,
):
    dp, y, x = place()
    c = y * COLS + x
    peers = [(x + j) % COLS for j in range(1, COLS)]
    above = (dp, ((y + 1) % ROWS) * COLS + x)
    below = (dp, ((y + ROWS - 1) % ROWS) * COLS + x)
    in_row = [(dp, y * COLS + p) for p in peers]
    fold = [(dp, flip(y, bit) * COLS + x) for bit in (1, 2, 4)]
    deep = [(dp + j) % DP for j in range(1, DP)]
    load = pltpu.make_async_copy(part, part_v, load_sem.at[0])
    load.start()
    greet(in_row + [above, below] + fold[1:] + [(to, c) for to in deep])
    before = {}
    started = []

    def hop(step, n, way):
        first = n if way == 0 else 1 - n
        land, stage, ss, rs, to = (
            (down, down_out, dn_s, dn_r, below), (up, up_out, up_s, up_r, above),
        )[way]
        owner = (y + ROWS - 4 + step) % ROWS if way == 0 else (y + 4 - step) % ROWS
        if step == first:
            src = part.at[owner, n]
        else:
            before[way, n].wait_recv()
            stage[step, n] = (
                land[step - 1, n].astype(jnp.float32) + part_v[owner, n].astype(jnp.float32)
            ).astype(jnp.bfloat16)
            src = stage.at[step, n]
        before[way, n] = send(src, land.at[step, n], ss.at[step, n], rs.at[step, n], to)
        started.append(before[way, n])

    hop(0, 0, 0)
    hop(0, 1, 1)
    hop(1, 1, 0)
    hop(1, 0, 1)
    own_q = pltpu.make_async_copy(dqh.at[x], dq.at[:, cols(x * GW, GW)], own_sem.at[0])
    own_q.start()
    back = [
        send(dqh.at[p], dq.at[:, cols(x * GW, GW)], q_s.at[j], q_r.at[j], in_row[j])
        for j, p in enumerate(peers)
    ]
    totals[0] = biasp[...]
    folds = []

    def fold_next():
        n = len(folds)
        if n:
            folds[-1].wait_recv()
            totals[n] = totals[n - 1] + inbox[n - 1]
        if n < len(fold):
            folds.append(send(totals.at[n], inbox.at[n], b_s.at[n], b_r.at[n], fold[n]))

    fold_next()
    load.wait()
    hop(1, 0, 0)
    hop(1, 1, 1)
    fold_next()
    hop(2, 1, 0)
    hop(2, 0, 1)
    fold_next()
    hop(2, 0, 0)
    hop(2, 1, 1)
    fold_next()
    bx[x] = totals[len(fold)]
    wide = [send(bx.at[x], bx.at[x], x_s.at[j], x_r.at[j], t) for j, t in enumerate(in_row)]
    hop(3, 1, 0)
    hop(3, 0, 1)
    for copy in wide:
        copy.wait()
    across = [
        send(bx.at[(to % 8) // 2], bd.at[dp], d_s.at[j], d_r.at[j], (to, c))
        for j, to in enumerate(deep)
    ]
    bd[dp] = bx[(dp % 8) // 2]
    hop(3, 0, 0)
    hop(3, 1, 1)
    last = []
    for n, dst in ((1, dkv_v), (0, dkv_k)):
        before[0, n].wait_recv()
        before[1, n].wait_recv()
        total = (
            part_v[y, n].astype(jnp.float32)
            + down[3, n].astype(jnp.float32)
            + up[3, n].astype(jnp.float32)
        )
        final[n] = total.astype(jnp.bfloat16).reshape(COLS, BLK, D)
        for j, p in enumerate(peers):
            last.append(
                send(final.at[n, j + 1], dst.at[:, cols(x * D, D)], f_s.at[j, n], f_r.at[j, n], in_row[j])
            )
        last_own = pltpu.make_async_copy(
            final.at[n, 0], dst.at[:, cols(x * D, D)], own_sem.at[1 + n]
        )
        last_own.start()
        last.append(last_own)
    for copy in started + folds:
        copy.wait_send()
    for copy in back:
        copy.wait()
    own_q.wait()
    for copy in last + across:
        copy.wait()
    entry = jnp.sum(bd[...], axis=0)
    picked = jnp.where(dp < 8, entry[0:1], entry[1:2])
    swapped = jnp.concatenate([picked[:, 64:], picked[:, :64]], axis=1)
    bias[...] = jnp.where(dp % 2 == 0, picked, swapped)


def give_back(part, biasp, dqh):
    bf = jnp.bfloat16
    f32 = jnp.float32
    sem = pltpu.SemaphoreType.DMA
    rows = COLS * BLK
    land = ((4, 2, rows, D), bf)
    scratch = [
        ((ROWS, 2, rows, D), bf), land, land, land, land, ((2, COLS, BLK, D), bf),
        ((4, 8, D), f32), ((3, 8, D), f32), ((COLS, 8, D), f32), ((DP, 8, D), f32),
    ]
    outs = (((BLK, KV * GW), bf), ((BLK, KV * D), bf), ((BLK, KV * D), bf), ((1, D), f32))
    return pl.pallas_call(
        give_back_kernel,
        out_shape=tuple(jax.ShapeDtypeStruct(*s) for s in outs),
        in_specs=[ANY, VMEM, ANY],
        out_specs=[ANY, ANY, ANY, VMEM],
        scratch_shapes=[pltpu.VMEM(*s) for s in scratch] + [
            sem((1,)), sem((3,)), sem((3,)), sem((3,)),
            sem((4, 2)), sem((4, 2)), sem((4, 2)), sem((4, 2)),
            sem((3, 2)), sem((3, 2)),
            sem((3,)), sem((3,)), sem((3,)), sem((3,)), sem((15,)), sem((15,)),
        ],
        compiler_params=pltpu.CompilerParams(
            collective_id=1, has_side_effects=True, vmem_limit_bytes=LIMIT
        ),
        name="give_back",
    )(part, biasp, dqh)


def store_kernel(dq, dk, dv, bias, dq_out, dk_out, dv_out, bias_out, dq_v, dk_v, dv_v, sem):
    moves = []
    for n in range(4):
        rows = pl.ds(n * 32, 32)
        moves.append((dq.at[rows], dq_v.at[rows], dq_out.at[rows]))
    moves.append((dk, dk_v, dk_out))
    moves.append((dv, dv_v, dv_out))
    first = [pltpu.make_async_copy(m[0], m[1], sem.at[0, n]) for n, m in enumerate(moves)]
    second = [pltpu.make_async_copy(m[1], m[2], sem.at[1, n]) for n, m in enumerate(moves)]
    for copy in first:
        copy.start()
    bias_out[...] = bias[0, :64]
    for one, two in zip(first, second):
        one.wait()
        two.start()
    for copy in second:
        copy.wait()


def store(dq, dk, dv, bias):
    shape = lambda a: jax.ShapeDtypeStruct(a.shape, a.dtype)
    return pl.pallas_call(
        store_kernel,
        out_shape=(shape(dq), shape(dk), shape(dv), jax.ShapeDtypeStruct((64,), jnp.float32)),
        in_specs=[ANY, ANY, ANY, VMEM],
        out_specs=[ANY, ANY, ANY, VMEM],
        scratch_shapes=[pltpu.VMEM(a.shape, a.dtype) for a in (dq, dk, dv)]
        + [pltpu.SemaphoreType.DMA((2, 6))],
        compiler_params=pltpu.CompilerParams(vmem_limit_bytes=LIMIT),
        name="store",
    )(dq, dk, dv, bias)


def on_device(queries, keys, values, outputs, d_out, log_sums, block_path, live_len):
    gathered = gather(
        block_path, live_len,
        queries[0], d_out[0], outputs[0], keys[0], values[0], jnp.transpose(log_sums, (1, 0, 2)),
    )
    qh, doh, stat, dqt_near, near, far, bias_near = gathered
    part, dqh, biasp = attend(
        block_path, live_len, qh, doh, stat, dqt_near, far, near, bias_near
    )
    dq, dk, dv, bias = store(*give_back(part, biasp, dqh))
    return dq[None], dk[None], dv[None], bias


def solution(mesh):
    wide = P("dp", "ctx", None)
    return jax.shard_map(
        on_device,
        mesh=mesh,
        in_specs=(wide, wide, wide, wide, wide, P("dp", None, "ctx"), P("dp", None), P("dp", None)),
        out_specs=(wide, wide, wide, P("dp")),
        check_vma=False,
    )
```

time: 122 us -> 105 us (0.86)
  the two profiles are of different devices: /device:TPU:2 before, /device:TPU:8 now
where the time goes in v2:
time: 105 us
  Pallas kernels  104 us (99%)
    pallas_call x1, Pallas kernels, give_back(): pl.pallas_call(give_back_kernel, out_shape=tuple((jax.ShapeDtypeStruct(*s...  55.5 us
    pallas_call x1, Pallas kernels, gather(): pl.pallas_call(gather_kernel, out_shape=tuple((jax.ShapeDtypeStruct(*s) f...  40.2 us
    pallas_call x1, Pallas kernels, attend(): pl.pallas_call(attend_kernel, out_shape=tuple((jax.ShapeDtypeStruct(*s) f...  5.06 us
    pallas_call x1, Pallas kernels, store(): pl.pallas_call(store_kernel, out_shape=(shape(dq), shape(dk), shape(dv),...  3.15 us

profile of v2, /device:TPU:8, one launch (start us, length us, event | category | flops | bytes accessed | tf_op | source)
XLA Modules:
  0.0 104.8 jit_solution(2497214277161292804)
XLA Ops:
  0.6 40.2 %gather.1 = (bf16[4,128,640]{2,1,0:T(8,128)(2,1)}, bf16[4,128,640]{2,1,0:T(8,128)(2,1)}, f32[4,16,128]{2,1,0:T(8,128)}, f32[4,128,640]{2,1,0:T(8,128)}, bf16[4,2...) custom-call(s32[1,32]{1,0:T(1,128)} %path.3, s32[1,32]{1,0:T(1,128)} %live.3, ...), custom_call_target="tpu_custom_call" | custom-call | tf_op jit(solution)/shard_map/gather/pallas_call | solution.py:334
  40.9 5.1 %attend.1 = (bf16[8,2,512,128]{3,2,1,0:T(8,128)(2,1)}, bf16[4,128,640]{2,1,0:T(8,128)(2,1)}, f32[8,128]{1,0:T(8,128)}) custom-call(s32[1,32]{1,0:T(1,128)} %path.3, s32[1,32]{1,0:T(1,128)} %live.3, bf16[4,128,640]{2,1,0:T(8,128)(2,1)} %get-tuple-element.22.qh, bf16[4,128,640]{2,1,0:T(8,128)(2,1)} %get-tuple-element.23.doh, ...), custom_call_target="tpu_custom_call" | custom-call | tf_op jit(solution)/shard_map/attend/pallas_call | solution.py:471
  46.0 55.5 %give_back.1 = (bf16[128,2560]{1,0:T(8,128)(2,1)}, bf16[128,512]{1,0:T(8,128)(2,1)}, bf16[128,512]{1,0:T(8,128)(2,1)}, f32[1,128]{1,0:T(1,128)}) custom-call(bf16[8,2,512,128]{3,2,1,0:T(8,128)(2,1)} %get-tuple-element.29.part, f32[8,128]{1,0:T(8,128)} %get-tuple-element.30.biasp, bf16[4,128,640]{2,1,0:T(8,128)(2,1)} %get-tuple-element.31.dqh), custom_call_target="tpu_custom_call" | custom-call | tf_op jit(solution)/shard_map/give_back/pallas_call | solution.py:611
  101.5 3.1 %store.1 = (bf16[128,2560]{1,0:T(8,128)(2,1)}, bf16[128,512]{1,0:T(8,128)(2,1)}, bf16[128,512]{1,0:T(8,128)(2,1)}, f32[64]{0:T(128)}) custom-call(bf16[128,2560]{1,0:T(8,128)(2,1)} %get-tuple-element.32.dq, bf16[128,512]{1,0:T(8,128)(2,1)} %get-tuple-element.33.dk, bf16[128,512]{1,0:T(8,128)(2,1)} %get-tuple-element.34.dv, f32[1,128]{1,0:T(1,128)} %get-tuple-element.35.bias), custom_call_target="tpu_custom_call" | custom-call | tf_op jit(solution)/shard_map/store/pallas_call | solution.py:650

commit v3 on v2

--- a/solution.py
+++ b/solution.py
@@ -253,10 +253,10 @@
     for copy in own_q:
         copy.wait()
     forward(1, 0)
+    move(1)
     own_pair(0)
     forward(1, 2)
     forward(1, 1)
-    move(1)
     last_pair(0)
     for j in (0, 2):
         stats[j].wait_recv()
@@ -479,15 +479,11 @@
     )(path, live, qh, doh, stat, dqt_near, far, near, bias_near)
 
 
-def flip(value, bit):
-    return value + bit - 2 * bit * ((value // bit) % 2)
-
-
 def give_back_kernel(
     part, biasp, dqh,
     dq, dkv_k, dkv_v, bias,
-    part_v, down, up, down_out, up_out, final, totals, inbox, bx, bd,
-    load_sem, own_sem, q_s, q_r, dn_s, dn_r, up_s, up_r, f_s, f_r, b_s, b_r, x_s, x_r, d_s, d_r,
+    part_v, down, up, down_out, up_out, final, by, bx, twin, bz,
+    load_sem, own_sem, q_s, q_r, dn_s, dn_r, up_s, up_r, f_s, f_r, y_s, y_r, x_s, x_r, t_s, t_r, d_s, d_r,
 ):
     dp, y, x = place()
     c = y * COLS + x
@@ -495,11 +491,13 @@
     above = (dp, ((y + 1) % ROWS) * COLS + x)
     below = (dp, ((y + ROWS - 1) % ROWS) * COLS + x)
     in_row = [(dp, y * COLS + p) for p in peers]
-    fold = [(dp, flip(y, bit) * COLS + x) for bit in (1, 2, 4)]
-    deep = [(dp + j) % DP for j in range(1, DP)]
+    in_col = [(dp, ((y + j) % ROWS) * COLS + x) for j in range(1, ROWS)]
+    core, z = dp % 2, dp // 2
+    other = (dp + 1 - 2 * core, c)
+    deep = [((z + j) % 8) * 2 + core for j in range(1, 8)]
     load = pltpu.make_async_copy(part, part_v, load_sem.at[0])
     load.start()
-    greet(in_row + [above, below] + fold[1:] + [(to, c) for to in deep])
+    greet(in_row + in_col + [other] + [(to, c) for to in deep])
     before = {}
     started = []
 
@@ -530,41 +528,33 @@
         send(dqh.at[p], dq.at[:, cols(x * GW, GW)], q_s.at[j], q_r.at[j], in_row[j])
         for j, p in enumerate(peers)
     ]
-    totals[0] = biasp[...]
-    folds = []
-
-    def fold_next():
-        n = len(folds)
-        if n:
-            folds[-1].wait_recv()
-            totals[n] = totals[n - 1] + inbox[n - 1]
-        if n < len(fold):
-            folds.append(send(totals.at[n], inbox.at[n], b_s.at[n], b_r.at[n], fold[n]))
-
-    fold_next()
+    by[y] = biasp[...]
+    col = [send(by.at[y], by.at[y], y_s.at[j], y_r.at[j], t) for j, t in enumerate(in_col)]
     load.wait()
     hop(1, 0, 0)
     hop(1, 1, 1)
-    fold_next()
     hop(2, 1, 0)
     hop(2, 0, 1)
-    fold_next()
     hop(2, 0, 0)
     hop(2, 1, 1)
-    fold_next()
-    bx[x] = totals[len(fold)]
+    for copy in col:
+        copy.wait_recv()
+    bx[x] = jnp.sum(by[...], axis=0)
     wide = [send(bx.at[x], bx.at[x], x_s.at[j], x_r.at[j], t) for j, t in enumerate(in_row)]
     hop(3, 1, 0)
     hop(3, 0, 1)
     for copy in wide:
         copy.wait()
-    across = [
-        send(bx.at[(to % 8) // 2], bd.at[dp], d_s.at[j], d_r.at[j], (to, c))
-        for j, to in enumerate(deep)
-    ]
-    bd[dp] = bx[(dp % 8) // 2]
+    swap = send(bx, twin, t_s.at[0], t_r.at[0], other)
     hop(3, 0, 0)
     hop(3, 1, 1)
+    swap.wait()
+    twin[...] += bx[...]
+    across = [
+        send(twin.at[(to % 8) // 2], bz.at[z], d_s.at[j], d_r.at[j], (to, c))
+        for j, to in enumerate(deep)
+    ]
+    bz[z] = twin[(dp % 8) // 2]
     last = []
     for n, dst in ((1, dkv_v), (0, dkv_k)):
         before[0, n].wait_recv()
@@ -584,17 +574,17 @@
         )
         last_own.start()
         last.append(last_own)
-    for copy in started + folds:
-        copy.wait_send()
-    for copy in back:
+    for copy in across:
         copy.wait()
-    own_q.wait()
-    for copy in last + across:
-        copy.wait()
-    entry = jnp.sum(bd[...], axis=0)
+    entry = jnp.sum(bz[...], axis=0)
     picked = jnp.where(dp < 8, entry[0:1], entry[1:2])
     swapped = jnp.concatenate([picked[:, 64:], picked[:, :64]], axis=1)
     bias[...] = jnp.where(dp % 2 == 0, picked, swapped)
+    for copy in started + col:
+        copy.wait_send()
+    for copy in back + last:
+        copy.wait()
+    own_q.wait()
 
 
 def give_back(part, biasp, dqh):
@@ -605,7 +595,7 @@
     land = ((4, 2, rows, D), bf)
     scratch = [
         ((ROWS, 2, rows, D), bf), land, land, land, land, ((2, COLS, BLK, D), bf),
-        ((4, 8, D), f32), ((3, 8, D), f32), ((COLS, 8, D), f32), ((DP, 8, D), f32),
+        ((ROWS, 8, D), f32), ((COLS, 8, D), f32), ((COLS, 8, D), f32), ((8, 8, D), f32),
     ]
     outs = (((BLK, KV * GW), bf), ((BLK, KV * D), bf), ((BLK, KV * D), bf), ((1, D), f32))
     return pl.pallas_call(
@@ -617,7 +607,7 @@
             sem((1,)), sem((3,)), sem((3,)), sem((3,)),
             sem((4, 2)), sem((4, 2)), sem((4, 2)), sem((4, 2)),
             sem((3, 2)), sem((3, 2)),
-            sem((3,)), sem((3,)), sem((3,)), sem((3,)), sem((15,)), sem((15,)),
+            sem((7,)), sem((7,)), sem((3,)), sem((3,)), sem((1,)), sem((1,)), sem((7,)), sem((7,)),
         ],
         compiler_params=pltpu.CompilerParams(
             collective_id=1, has_side_effects=True, vmem_limit_bytes=LIMIT

time: 105 us -> 99.3 us (0.946)
  Pallas kernels: 104 us -> 97.8 us
    pallas_call x1, Pallas kernels: 55.5 us -> 49.3 us  [give_back(): pl.pallas_call(give_back_kernel, out_shape=tuple((jax.ShapeDtypeStruct(*s...]
where the time goes in v3:
time: 99.3 us; the launch traced here: 98.6 us
  Pallas kernels  97.8 us (98%)
    pallas_call x1, Pallas kernels, give_back(): pl.pallas_call(give_back_kernel, out_shape=tuple((jax.ShapeDtypeStruct(*s...  49.3 us
    pallas_call x1, Pallas kernels, gather(): pl.pallas_call(gather_kernel, out_shape=tuple((jax.ShapeDtypeStruct(*s) f...  40.3 us
    pallas_call x1, Pallas kernels, attend(): pl.pallas_call(attend_kernel, out_shape=tuple((jax.ShapeDtypeStruct(*s) f...  5.06 us
    pallas_call x1, Pallas kernels, store(): pl.pallas_call(store_kernel, out_shape=(shape(dq), shape(dk), shape(dv),...  3.15 us

profile of v3, /device:TPU:8, one launch (start us, length us, event | category | flops | bytes accessed | tf_op | source)
XLA Modules:
  0.0 98.6 jit_solution(1471233463897163332)
XLA Ops:
  0.6 40.3 %gather.1 = (bf16[4,128,640]{2,1,0:T(8,128)(2,1)}, bf16[4,128,640]{2,1,0:T(8,128)(2,1)}, f32[4,16,128]{2,1,0:T(8,128)}, f32[4,128,640]{2,1,0:T(8,128)}, bf16[4,2...) custom-call(s32[1,32]{1,0:T(1,128)} %path.3, s32[1,32]{1,0:T(1,128)} %live.3, ...), custom_call_target="tpu_custom_call" | custom-call | tf_op jit(solution)/shard_map/gather/pallas_call | solution.py:334
  41.0 5.1 %attend.1 = (bf16[8,2,512,128]{3,2,1,0:T(8,128)(2,1)}, bf16[4,128,640]{2,1,0:T(8,128)(2,1)}, f32[8,128]{1,0:T(8,128)}) custom-call(s32[1,32]{1,0:T(1,128)} %path.3, s32[1,32]{1,0:T(1,128)} %live.3, bf16[4,128,640]{2,1,0:T(8,128)(2,1)} %get-tuple-element.22.qh, bf16[4,128,640]{2,1,0:T(8,128)(2,1)} %get-tuple-element.23.doh, ...), custom_call_target="tpu_custom_call" | custom-call | tf_op jit(solution)/shard_map/attend/pallas_call | solution.py:471
  46.0 49.3 %give_back.1 = (bf16[128,2560]{1,0:T(8,128)(2,1)}, bf16[128,512]{1,0:T(8,128)(2,1)}, bf16[128,512]{1,0:T(8,128)(2,1)}, f32[1,128]{1,0:T(1,128)}) custom-call(bf16[8,2,512,128]{3,2,1,0:T(8,128)(2,1)} %get-tuple-element.29.part, f32[8,128]{1,0:T(8,128)} %get-tuple-element.30.biasp, bf16[4,128,640]{2,1,0:T(8,128)(2,1)} %get-tuple-element.31.dqh), custom_call_target="tpu_custom_call" | custom-call | tf_op jit(solution)/shard_map/give_back/pallas_call | solution.py:601
  95.3 3.1 %store.1 = (bf16[128,2560]{1,0:T(8,128)(2,1)}, bf16[128,512]{1,0:T(8,128)(2,1)}, bf16[128,512]{1,0:T(8,128)(2,1)}, f32[64]{0:T(128)}) custom-call(bf16[128,2560]{1,0:T(8,128)(2,1)} %get-tuple-element.32.dq, bf16[128,512]{1,0:T(8,128)(2,1)} %get-tuple-element.33.dk, bf16[128,512]{1,0:T(8,128)(2,1)} %get-tuple-element.34.dv, f32[1,128]{1,0:T(1,128)} %get-tuple-element.35.bias), custom_call_target="tpu_custom_call" | custom-call | tf_op jit(solution)/shard_map/store/pallas_call | solution.py:640

commit v4 on v3

--- a/solution.py
+++ b/solution.py
@@ -62,7 +62,7 @@
     return copy
 
 
-def unit(i, b, row, x, path, kc, vc, qref, gref, stat, dk_at, dv_at, dqt):
+def unit(i, b, row, x, path, kc, vc, qref, gref, stat, dk_at, dv_at, dqt, span=1):
     heads = lambda a: jnp.concatenate([a[:, n * D : (n + 1) * D] for n in range(GROUP)], axis=0)
     flat = lambda first: jnp.concatenate(
         [stat[i, first + n : first + n + 1, :] for n in range(GROUP)], axis=1
@@ -76,8 +76,8 @@
         lax.broadcasted_iota(jnp.int32, (BLK, GW), 1) % BLK
     )
     p_low, ds = [], []
-    for j in range(COLS):
-        kb = row * COLS + (x + j) % COLS
+    for j in range(COLS * span):
+        kb = (row + j // COLS) * COLS + (x + j) % COLS
         theirs = path[0, kb]
         joined = (theirs == 0) | (theirs == mine) | (mine == 0)
         shift = base + jnp.where(joined, 0.0, FAR)
@@ -88,8 +88,8 @@
         ds.append((p * (t[at] - delta)).astype(jnp.bfloat16))
     p_low = jnp.concatenate(p_low, axis=0)
     ds = jnp.concatenate(ds, axis=0)
-    dk_at[...] += dot(ds, qs)
-    dv_at[...] += dot(p_low, gs)
+    dk_at[...] += dot(ds, qs).reshape(dk_at.shape)
+    dv_at[...] += dot(p_low, gs).reshape(dv_at.shape)
     dqt[i] += dot(kc, ds, TN)
 
 
@@ -422,7 +422,19 @@
 
                 return 0
 
-            lax.fori_loop(lower, upper, one, 0)
+            def two(n, _):
+                at = pl.ds(lower + 2 * n, 2)
+                wide = (2 * COLS * BLK, D)
+                unit(
+                    i, b, lower + 2 * n, x, path,
+                    far_v[at, 0].reshape(wide), far_v[at, 1].reshape(wide),
+                    q_v, g_v, stat_v, dk.at[at], dv.at[at], dqt, 2,
+                )
+                return 0
+
+            twos = jnp.where(mine == 0, (upper - lower) // 2, 0)
+            lax.fori_loop(0, twos, two, 0)
+            lax.fori_loop(lower + 2 * twos, upper, one, 0)
             return 0
 
         lax.fori_loop(0, COLS, query, 0)

time: 99.3 us -> 98.9 us (level)
  no operation moved by 1% of the time
where the time goes in v4:
time: 98.9 us; the launch traced here: 98.6 us
  Pallas kernels  97.8 us (99%)
    pallas_call x1, Pallas kernels, give_back(): pl.pallas_call(give_back_kernel, out_shape=tuple((jax.ShapeDtypeStruct(*s...  49.2 us
    pallas_call x1, Pallas kernels, gather(): pl.pallas_call(gather_kernel, out_shape=tuple((jax.ShapeDtypeStruct(*s) f...  40.3 us
    pallas_call x1, Pallas kernels, attend(): pl.pallas_call(attend_kernel, out_shape=tuple((jax.ShapeDtypeStruct(*s) f...  5.06 us
    pallas_call x1, Pallas kernels, store(): pl.pallas_call(store_kernel, out_shape=(shape(dq), shape(dk), shape(dv),...  3.15 us

profile of v4, /device:TPU:8, one launch (start us, length us, event | category | flops | bytes accessed | tf_op | source)
XLA Modules:
  0.0 98.6 jit_solution(17146214126790993066)
XLA Ops:
  0.6 40.3 %gather.1 = (bf16[4,128,640]{2,1,0:T(8,128)(2,1)}, bf16[4,128,640]{2,1,0:T(8,128)(2,1)}, f32[4,16,128]{2,1,0:T(8,128)}, f32[4,128,640]{2,1,0:T(8,128)}, bf16[4,2...) custom-call(s32[1,32]{1,0:T(1,128)} %path.3, s32[1,32]{1,0:T(1,128)} %live.3, ...), custom_call_target="tpu_custom_call" | custom-call | tf_op jit(solution)/shard_map/gather/pallas_call | solution.py:334
  41.0 5.1 %attend.1 = (bf16[8,2,512,128]{3,2,1,0:T(8,128)(2,1)}, bf16[4,128,640]{2,1,0:T(8,128)(2,1)}, f32[8,128]{1,0:T(8,128)}) custom-call(s32[1,32]{1,0:T(1,128)} %path.3, s32[1,32]{1,0:T(1,128)} %live.3, bf16[4,128,640]{2,1,0:T(8,128)(2,1)} %get-tuple-element.22.qh, bf16[4,128,640]{2,1,0:T(8,128)(2,1)} %get-tuple-element.23.doh, ...), custom_call_target="tpu_custom_call" | custom-call | tf_op jit(solution)/shard_map/attend/pallas_call | solution.py:483
  46.0 49.2 %give_back.1 = (bf16[128,2560]{1,0:T(8,128)(2,1)}, bf16[128,512]{1,0:T(8,128)(2,1)}, bf16[128,512]{1,0:T(8,128)(2,1)}, f32[1,128]{1,0:T(1,128)}) custom-call(bf16[8,2,512,128]{3,2,1,0:T(8,128)(2,1)} %get-tuple-element.29.part, f32[8,128]{1,0:T(8,128)} %get-tuple-element.30.biasp, bf16[4,128,640]{2,1,0:T(8,128)(2,1)} %get-tuple-element.31.dqh), custom_call_target="tpu_custom_call" | custom-call | tf_op jit(solution)/shard_map/give_back/pallas_call | solution.py:613
  95.3 3.1 %store.1 = (bf16[128,2560]{1,0:T(8,128)(2,1)}, bf16[128,512]{1,0:T(8,128)(2,1)}, bf16[128,512]{1,0:T(8,128)(2,1)}, f32[64]{0:T(128)}) custom-call(bf16[128,2560]{1,0:T(8,128)(2,1)} %get-tuple-element.32.dq, bf16[128,512]{1,0:T(8,128)(2,1)} %get-tuple-element.33.dk, bf16[128,512]{1,0:T(8,128)(2,1)} %get-tuple-element.34.dv, f32[1,128]{1,0:T(1,128)} %get-tuple-element.35.bias), custom_call_target="tpu_custom_call" | custom-call | tf_op jit(solution)/shard_map/store/pallas_call | solution.py:652
